TPU v7x, 32 devices: a whole 2x2x4 slice. The times are simulated.
32 devices in a mesh: wide: 16 (over z, y, core), narrow: 2 (over x).
Axes of the slice: x: 2, y: 2, z: 4, core: 2. Of those that a mesh axis runs over, the one named last changes fastest.
Arguments:
- target_input: bfloat16 [64, 128, 1024], P(('wide', 'narrow')), may hold values from -6 to 6
- memory: bfloat16 [64, 1024, 1024], P(('wide', 'narrow')), may hold values from -6 to 6
- cotangent: bfloat16 [64, 128, 1024], P(('wide', 'narrow')), may hold values from -6 to 6
- mem_lengths: int32 [64], P(('wide', 'narrow')), may hold values from 300 to 1024, as said below
- tgt_lengths: int32 [64], P(('wide', 'narrow')), may hold values from 32 to 128, as said below
- self_qkv: bfloat16 [1024, 3072], P(('wide', 'narrow')), may hold values from -0.1875 to 0.1875
- self_out: bfloat16 [1024, 1024], P(('wide', 'narrow')), may hold values from -0.75 to 0.75
- self_bias: bfloat16 [3, 1024], P(None, ('wide', 'narrow')), may hold values from -3 to 3
- norm1_gain: bfloat16 [1024], P(('wide', 'narrow')), may hold values from 0.5 to 1.5
- norm1_shift: bfloat16 [1024], P(('wide', 'narrow')), may hold values from -3 to 3
- cross_qkv: bfloat16 [1024, 3072], P(('wide', 'narrow')), may hold values from -0.1875 to 0.1875
- cross_out: bfloat16 [1024, 1024], P(('wide', 'narrow')), may hold values from -3 to 3
- cross_bias: bfloat16 [3, 1024], P(None, ('wide', 'narrow')), may hold values from -3 to 3
- norm2_gain: bfloat16 [1024], P(('wide', 'narrow')), may hold values from 0.5 to 1.5
- norm2_shift: bfloat16 [1024], P(('wide', 'narrow')), may hold values from -3 to 3
- ffn_up: bfloat16 [1024, 4096], P(('wide', 'narrow')), may hold values from -0.1875 to 0.1875
- up_bias: bfloat16 [4096], P(('wide', 'narrow')), may hold values from -3 to 3
- ffn_down: bfloat16 [4096, 1024], P(('wide', 'narrow')), may hold values from -0.09375 to 0.09375
- down_bias: bfloat16 [1024], P(('wide', 'narrow')), may hold values from -3 to 3
- norm3_gain: bfloat16 [1024], P(('wide', 'narrow')), may hold values from 0.5 to 1.5
- norm3_shift: bfloat16 [1024], P(('wide', 'narrow')), may hold values from -3 to 3
Outputs:
- block_out: bfloat16 [64, 128, 1024], P(('wide', 'narrow'))
- target_grad: bfloat16 [64, 128, 1024], P(('wide', 'narrow'))
- memory_grad: bfloat16 [64, 1024, 1024], P(('wide', 'narrow'))
- self_qkv_grad: float32 [1024, 3072], P(('wide', 'narrow'))
- self_out_grad: float32 [1024, 1024], P(('wide', 'narrow'))
- self_bias_grad: float32 [3, 1024], P(None, ('wide', 'narrow'))
- norm1_gain_grad: float32 [1024], P(('wide', 'narrow'))
- norm1_shift_grad: float32 [1024], P(('wide', 'narrow'))
- cross_qkv_grad: float32 [1024, 3072], P(('wide', 'narrow'))
- cross_out_grad: float32 [1024, 1024], P(('wide', 'narrow'))
- cross_bias_grad: float32 [3, 1024], P(None, ('wide', 'narrow'))
- norm2_gain_grad: float32 [1024], P(('wide', 'narrow'))
- norm2_shift_grad: float32 [1024], P(('wide', 'narrow'))
- ffn_up_grad: float32 [1024, 4096], P(('wide', 'narrow'))
- up_bias_grad: float32 [4096], P(('wide', 'narrow'))
- ffn_down_grad: float32 [4096, 1024], P(('wide', 'narrow'))
- down_bias_grad: float32 [1024], P(('wide', 'narrow'))
- norm3_gain_grad: float32 [1024], P(('wide', 'narrow'))
- norm3_shift_grad: float32 [1024], P(('wide', 'narrow'))
Inputs may be any that keep to these rules, and one draw needn't show every extreme that they name: `mem_lengths`: at least one table has 1024 live positions. `tgt_lengths`: at least one sample has 128 live target positions.
All inputs are finite; a program needn't handle non-finite values.
Results may differ from a plain program's by a relative error of at most 0.02.
Values may be sent and summed in bfloat16 or wider, within the bound.
A program may use at most 256 MiB of HBM per device.

v0:
```python
import math

import jax
import jax.numpy as jnp
from jax import lax
from jax.sharding import PartitionSpec as P

H = 16
HD = 64


NORM_EPSILON = 1e-05
MASK_VALUE = -1e30


def column_products(left_side, right_side):
    return lax.dot_general(
        left_side, right_side, (((0,), (0,)), ((), ())), preferred_element_type=jnp.float32
    )


def times_transpose(left_side, right_side):
    return lax.dot_general(
        left_side, right_side, (((1,), (1,)), ((), ())), preferred_element_type=jnp.float32
    )


def row_sums(values):
    return jnp.sum(values.astype(jnp.float32), axis=0)


def norm_forward(summed, norm_gain, norm_shift):
    average = jnp.mean(summed, axis=-1, keepdims=True)
    centred = summed - average
    inverse = lax.rsqrt(jnp.mean(centred * centred, axis=-1, keepdims=True) + NORM_EPSILON)
    normed = centred * inverse
    return (normed * norm_gain + norm_shift, normed, inverse)


def norm_backward(incoming, normed, inverse, norm_gain):
    gain_grad = jnp.sum(incoming * normed, axis=0)
    shift_grad = jnp.sum(incoming, axis=0)
    scaled = incoming * norm_gain
    centred_grad = (
        scaled
        - jnp.mean(scaled, axis=-1, keepdims=True)
        - normed * jnp.mean(scaled * normed, axis=-1, keepdims=True)
    )
    return (centred_grad * inverse, gain_grad, shift_grad)


def gelu_parts(pre_act):
    normal_cdf = 0.5 * (1.0 + lax.erf(pre_act * (1.0 / math.sqrt(2.0))))
    density = jnp.exp(-0.5 * pre_act * pre_act) * (1.0 / math.sqrt(2.0 * math.pi))
    return (pre_act * normal_cdf, normal_cdf + pre_act * density)


def masked_scores(queries, key_rows, usable):
    scores = jnp.einsum("sqhe,skhe->shqk", queries, key_rows, preferred_element_type=jnp.float32)
    return jnp.where(usable[:, None], scores, MASK_VALUE)


def attend(queries, key_rows, values, usable):
    scores = masked_scores(queries, key_rows, usable)
    row_peak = jnp.max(scores, axis=-1, keepdims=True)
    exponentials = jnp.exp(scores - row_peak)
    row_total = jnp.sum(exponentials, axis=-1, keepdims=True)
    probs_low = (exponentials / row_total).astype(jnp.bfloat16)
    mixed_heads = jnp.einsum(
        "shqk,skhe->sqhe", probs_low, values, preferred_element_type=jnp.float32
    )
    return (mixed_heads, row_peak + jnp.log(row_total))


def attend_back(queries, key_rows, values, usable, log_totals, upstream):
    attn_probs = jnp.exp(masked_scores(queries, key_rows, usable) - log_totals)
    probs_low = attn_probs.astype(jnp.bfloat16)
    prob_grad = jnp.einsum("sqhe,skhe->shqk", upstream, values, preferred_element_type=jnp.float32)
    row_delta = jnp.sum(attn_probs * prob_grad, axis=-1, keepdims=True)
    score_grad = (attn_probs * (prob_grad - row_delta)).astype(jnp.bfloat16)
    query_grad = jnp.einsum(
        "shqk,skhe->sqhe", score_grad, key_rows, preferred_element_type=jnp.float32
    )
    key_grad = jnp.einsum(
        "shqk,sqhe->skhe", score_grad, queries, preferred_element_type=jnp.float32
    )
    value_grad = jnp.einsum(
        "shqk,sqhe->skhe", probs_low, upstream, preferred_element_type=jnp.float32
    )
    return (query_grad, key_grad, value_grad)


def shards(
    target_input,
    memory,
    cotangent,
    mem_lengths,
    tgt_lengths,
    self_qkv,
    self_out,
    self_bias,
    norm1_gain,
    norm1_shift,
    cross_qkv,
    cross_out,
    cross_bias,
    norm2_gain,
    norm2_shift,
    ffn_up,
    up_bias,
    ffn_down,
    down_bias,
    norm3_gain,
    norm3_shift,
):
    samples_dev, tgt_len, model_width = target_input.shape
    mem_len = memory.shape[1]
    score_scale = 1.0 / math.sqrt(HD)
    tgt_rows = samples_dev * tgt_len
    mem_rows = samples_dev * mem_len
    head_shape = (samples_dev, tgt_len, H, HD)
    mem_head_shape = (samples_dev, mem_len, H, HD)
    inputs_flat = target_input.reshape(tgt_rows, model_width)
    memory_flat = memory.reshape(mem_rows, model_width)
    positions = jnp.arange(tgt_len)
    self_usable = (positions[None, None, :] <= positions[None, :, None]) & (
        positions[None, None, :] < tgt_lengths[:, None, None]
    )
    cross_usable = jnp.arange(mem_len)[None, None, :] < mem_lengths[:, None, None]
    self_whole = (
        lax.all_gather(self_qkv, ("wide", "narrow"), axis=0, tiled=True),
        lax.all_gather(self_out, ("wide", "narrow"), axis=0, tiled=True),
        lax.all_gather(self_bias, ("wide", "narrow"), axis=1, tiled=True),
        lax.all_gather(norm1_gain, ("wide", "narrow"), axis=0, tiled=True),
        lax.all_gather(norm1_shift, ("wide", "narrow"), axis=0, tiled=True),
    )
    qkv_weight, out_weight, self_rows, gain_one, shift_one = self_whole
    self_shift = self_rows.astype(jnp.float32)
    projected = jnp.dot(inputs_flat, qkv_weight, preferred_element_type=jnp.float32)
    self_q = (
        ((projected[:, :model_width] + self_shift[0]) * score_scale)
        .astype(jnp.bfloat16)
        .reshape(head_shape)
    )
    self_k = projected[:, model_width : 2 * model_width].astype(jnp.bfloat16).reshape(head_shape)
    self_v = (
        (projected[:, 2 * model_width :] + self_shift[1]).astype(jnp.bfloat16).reshape(head_shape)
    )
    self_mixed, self_logsum = attend(self_q, self_k, self_v, self_usable)
    self_attn = self_mixed.reshape(tgt_rows, model_width).astype(jnp.bfloat16)
    self_branch = jnp.dot(self_attn, out_weight, preferred_element_type=jnp.float32) + self_shift[2]
    hidden_one, normed_one, inverse_one = norm_forward(
        inputs_flat.astype(jnp.float32) + self_branch,
        gain_one.astype(jnp.float32),
        shift_one.astype(jnp.float32),
    )
    hidden_one_low = hidden_one.astype(jnp.bfloat16)
    cross_whole = (
        lax.all_gather(cross_qkv, ("wide", "narrow"), axis=0, tiled=True),
        lax.all_gather(cross_out, ("wide", "narrow"), axis=0, tiled=True),
        lax.all_gather(cross_bias, ("wide", "narrow"), axis=1, tiled=True),
        lax.all_gather(norm2_gain, ("wide", "narrow"), axis=0, tiled=True),
        lax.all_gather(norm2_shift, ("wide", "narrow"), axis=0, tiled=True),
    )
    cross_in, cross_proj, cross_rows, gain_two, shift_two = cross_whole
    cross_shift = cross_rows.astype(jnp.float32)
    cross_q = (
        (
            (
                jnp.dot(
                    hidden_one_low, cross_in[:, :model_width], preferred_element_type=jnp.float32
                )
                + cross_shift[0]
            )
            * score_scale
        )
        .astype(jnp.bfloat16)
        .reshape(head_shape)
    )
    memory_kv = jnp.dot(memory_flat, cross_in[:, model_width:], preferred_element_type=jnp.float32)
    cross_k = memory_kv[:, :model_width].astype(jnp.bfloat16).reshape(mem_head_shape)
    cross_v = (
        (memory_kv[:, model_width:] + cross_shift[1]).astype(jnp.bfloat16).reshape(mem_head_shape)
    )
    cross_mixed, cross_logsum = attend(cross_q, cross_k, cross_v, cross_usable)
    cross_attn = cross_mixed.reshape(tgt_rows, model_width).astype(jnp.bfloat16)
    cross_branch = (
        jnp.dot(cross_attn, cross_proj, preferred_element_type=jnp.float32) + cross_shift[2]
    )
    hidden_two, normed_two, inverse_two = norm_forward(
        hidden_one + cross_branch, gain_two.astype(jnp.float32), shift_two.astype(jnp.float32)
    )
    hidden_two_low = hidden_two.astype(jnp.bfloat16)
    ffn_whole = (
        lax.all_gather(ffn_up, ("wide", "narrow"), axis=0, tiled=True),
        lax.all_gather(up_bias, ("wide", "narrow"), axis=0, tiled=True),
        lax.all_gather(ffn_down, ("wide", "narrow"), axis=0, tiled=True),
        lax.all_gather(down_bias, ("wide", "narrow"), axis=0, tiled=True),
        lax.all_gather(norm3_gain, ("wide", "narrow"), axis=0, tiled=True),
        lax.all_gather(norm3_shift, ("wide", "narrow"), axis=0, tiled=True),
    )
    up_weight, up_shift, down_weight, down_shift, gain_three, shift_three = ffn_whole
    pre_act = jnp.dot(
        hidden_two_low, up_weight, preferred_element_type=jnp.float32
    ) + up_shift.astype(jnp.float32)
    activated, gelu_slope = gelu_parts(pre_act)
    act_low = activated.astype(jnp.bfloat16)
    ffn_branch = jnp.dot(
        act_low, down_weight, preferred_element_type=jnp.float32
    ) + down_shift.astype(jnp.float32)
    result, normed_three, inverse_three = norm_forward(
        hidden_two + ffn_branch, gain_three.astype(jnp.float32), shift_three.astype(jnp.float32)
    )
    block_out = result.astype(jnp.bfloat16).reshape(samples_dev, tgt_len, model_width)
    ffn_back = (
        lax.all_gather(ffn_up, ("wide", "narrow"), axis=0, tiled=True),
        lax.all_gather(up_bias, ("wide", "narrow"), axis=0, tiled=True),
        lax.all_gather(ffn_down, ("wide", "narrow"), axis=0, tiled=True),
        lax.all_gather(down_bias, ("wide", "narrow"), axis=0, tiled=True),
        lax.all_gather(norm3_gain, ("wide", "narrow"), axis=0, tiled=True),
        lax.all_gather(norm3_shift, ("wide", "narrow"), axis=0, tiled=True),
    )
    up_weight, up_shift, down_weight, down_shift, gain_three, shift_three = ffn_back
    upstream = cotangent.reshape(tgt_rows, model_width).astype(jnp.float32)
    d_sum3, gain3_grad, shift3_grad = norm_backward(
        upstream, normed_three, inverse_three, gain_three.astype(jnp.float32)
    )
    d_ffn = d_sum3.astype(jnp.bfloat16)
    down_grad = column_products(act_low, d_ffn)
    down_shift_grad = row_sums(d_ffn)
    d_pre = (times_transpose(d_ffn, down_weight) * gelu_slope).astype(jnp.bfloat16)
    up_grad = column_products(hidden_two_low, d_pre)
    up_shift_grad = row_sums(d_pre)
    d_hidden2 = d_sum3 + times_transpose(d_pre, up_weight)
    ffn_parts = (
        lax.psum_scatter(up_grad, ("wide", "narrow"), scatter_dimension=0, tiled=True),
        lax.psum_scatter(up_shift_grad, ("wide", "narrow"), scatter_dimension=0, tiled=True),
        lax.psum_scatter(down_grad, ("wide", "narrow"), scatter_dimension=0, tiled=True),
        lax.psum_scatter(down_shift_grad, ("wide", "narrow"), scatter_dimension=0, tiled=True),
        lax.psum_scatter(gain3_grad, ("wide", "narrow"), scatter_dimension=0, tiled=True),
        lax.psum_scatter(shift3_grad, ("wide", "narrow"), scatter_dimension=0, tiled=True),
    )
    cross_back = (
        lax.all_gather(cross_qkv, ("wide", "narrow"), axis=0, tiled=True),
        lax.all_gather(cross_out, ("wide", "narrow"), axis=0, tiled=True),
        lax.all_gather(cross_bias, ("wide", "narrow"), axis=1, tiled=True),
        lax.all_gather(norm2_gain, ("wide", "narrow"), axis=0, tiled=True),
        lax.all_gather(norm2_shift, ("wide", "narrow"), axis=0, tiled=True),
    )
    cross_in, cross_proj, cross_rows, gain_two, shift_two = cross_back
    d_sum2, gain2_grad, shift2_grad = norm_backward(
        d_hidden2, normed_two, inverse_two, gain_two.astype(jnp.float32)
    )
    d_cross = d_sum2.astype(jnp.bfloat16)
    cross_proj_grad = column_products(cross_attn, d_cross)
    d_cross_attn = times_transpose(d_cross, cross_proj).astype(jnp.bfloat16).reshape(head_shape)
    cross_q_grad, cross_k_grad, cross_v_grad = attend_back(
        cross_q, cross_k, cross_v, cross_usable, cross_logsum, d_cross_attn
    )
    d_cross_q = (cross_q_grad * score_scale).astype(jnp.bfloat16).reshape(tgt_rows, model_width)
    d_cross_kv = jnp.concatenate(
        [cross_k_grad.reshape(mem_rows, model_width), cross_v_grad.reshape(mem_rows, model_width)],
        axis=1,
    ).astype(jnp.bfloat16)
    cross_in_grad = jnp.concatenate(
        [column_products(hidden_one_low, d_cross_q), column_products(memory_flat, d_cross_kv)],
        axis=1,
    )
    cross_shift_grad = jnp.stack(
        [row_sums(d_cross_q), row_sums(d_cross_kv[:, model_width:]), row_sums(d_cross)]
    )
    memory_grad = (
        times_transpose(d_cross_kv, cross_in[:, model_width:])
        .astype(jnp.bfloat16)
        .reshape(samples_dev, mem_len, model_width)
    )
    d_hidden1 = d_sum2 + times_transpose(d_cross_q, cross_in[:, :model_width])
    cross_parts = (
        lax.psum_scatter(cross_in_grad, ("wide", "narrow"), scatter_dimension=0, tiled=True),
        lax.psum_scatter(cross_proj_grad, ("wide", "narrow"), scatter_dimension=0, tiled=True),
        lax.psum_scatter(cross_shift_grad, ("wide", "narrow"), scatter_dimension=1, tiled=True),
        lax.psum_scatter(gain2_grad, ("wide", "narrow"), scatter_dimension=0, tiled=True),
        lax.psum_scatter(shift2_grad, ("wide", "narrow"), scatter_dimension=0, tiled=True),
    )
    self_back = (
        lax.all_gather(self_qkv, ("wide", "narrow"), axis=0, tiled=True),
        lax.all_gather(self_out, ("wide", "narrow"), axis=0, tiled=True),
        lax.all_gather(self_bias, ("wide", "narrow"), axis=1, tiled=True),
        lax.all_gather(norm1_gain, ("wide", "narrow"), axis=0, tiled=True),
        lax.all_gather(norm1_shift, ("wide", "narrow"), axis=0, tiled=True),
    )
    qkv_weight, out_weight, self_rows, gain_one, shift_one = self_back
    d_sum1, gain1_grad, shift1_grad = norm_backward(
        d_hidden1, normed_one, inverse_one, gain_one.astype(jnp.float32)
    )
    d_self = d_sum1.astype(jnp.bfloat16)
    self_out_part = column_products(self_attn, d_self)
    d_self_attn = times_transpose(d_self, out_weight).astype(jnp.bfloat16).reshape(head_shape)
    self_q_grad, self_k_grad, self_v_grad = attend_back(
        self_q, self_k, self_v, self_usable, self_logsum, d_self_attn
    )
    d_self_qkv = jnp.concatenate(
        [
            (self_q_grad * score_scale).reshape(tgt_rows, model_width),
            self_k_grad.reshape(tgt_rows, model_width),
            self_v_grad.reshape(tgt_rows, model_width),
        ],
        axis=1,
    ).astype(jnp.bfloat16)
    self_qkv_part = column_products(inputs_flat, d_self_qkv)
    self_shift_grad = jnp.stack(
        [
            row_sums(d_self_qkv[:, :model_width]),
            row_sums(d_self_qkv[:, 2 * model_width :]),
            row_sums(d_self),
        ]
    )
    target_grad = (
        (d_sum1 + times_transpose(d_self_qkv, qkv_weight))
        .astype(jnp.bfloat16)
        .reshape(samples_dev, tgt_len, model_width)
    )
    self_parts = (
        lax.psum_scatter(self_qkv_part, ("wide", "narrow"), scatter_dimension=0, tiled=True),
        lax.psum_scatter(self_out_part, ("wide", "narrow"), scatter_dimension=0, tiled=True),
        lax.psum_scatter(self_shift_grad, ("wide", "narrow"), scatter_dimension=1, tiled=True),
        lax.psum_scatter(gain1_grad, ("wide", "narrow"), scatter_dimension=0, tiled=True),
        lax.psum_scatter(shift1_grad, ("wide", "narrow"), scatter_dimension=0, tiled=True),
    )
    return (
        block_out,
        target_grad,
        memory_grad,
        self_parts[0],
        self_parts[1],
        self_parts[2],
        self_parts[3],
        self_parts[4],
        cross_parts[0],
        cross_parts[1],
        cross_parts[2],
        cross_parts[3],
        cross_parts[4],
        ffn_parts[0],
        ffn_parts[1],
        ffn_parts[2],
        ffn_parts[3],
        ffn_parts[4],
        ffn_parts[5],
    )


def solution(mesh):
    return jax.shard_map(
        shards,
        mesh=mesh,
        in_specs=(
            P(("wide", "narrow"), None, None),
            P(("wide", "narrow"), None, None),
            P(("wide", "narrow"), None, None),
            P(("wide", "narrow")),
            P(("wide", "narrow")),
            P(("wide", "narrow"), None),
            P(("wide", "narrow"), None),
            P(None, ("wide", "narrow")),
            P(("wide", "narrow")),
            P(("wide", "narrow")),
            P(("wide", "narrow"), None),
            P(("wide", "narrow"), None),
            P(None, ("wide", "narrow")),
            P(("wide", "narrow")),
            P(("wide", "narrow")),
            P(("wide", "narrow"), None),
            P(("wide", "narrow")),
            P(("wide", "narrow"), None),
            P(("wide", "narrow")),
            P(("wide", "narrow")),
            P(("wide", "narrow")),
        ),
        out_specs=(
            P(("wide", "narrow"), None, None),
            P(("wide", "narrow"), None, None),
            P(("wide", "narrow"), None, None),
            P(("wide", "narrow"), None),
            P(("wide", "narrow"), None),
            P(None, ("wide", "narrow")),
            P(("wide", "narrow")),
            P(("wide", "narrow")),
            P(("wide", "narrow"), None),
            P(("wide", "narrow"), None),
            P(None, ("wide", "narrow")),
            P(("wide", "narrow")),
            P(("wide", "narrow")),
            P(("wide", "narrow"), None),
            P(("wide", "narrow")),
            P(("wide", "narrow"), None),
            P(("wide", "narrow")),
            P(("wide", "narrow")),
            P(("wide", "narrow")),
        ),
        check_vma=False,
    )
```

profile of v0, /device:TPU:4, one launch (start us, length us, event | category | flops | bytes accessed | tf_op | source)
XLA Modules:
  0.0 2120.1 jit_solution(337869315326066520)
XLA Ops:
  17.1 41.6 %all-reduce.16 = (bf16[1024]{0:T(1024)(128)(2,1)S(1)}, bf16[1024]{0:T(1024)(128)(2,1)S(1)}, bf16[1024]{0:T(1024)(128)(2,1)S(1)}, bf16[1024]{0:T(1024)(128)(2,1)S...) all-reduce(bf16[1024]{0:T(1024)(128)(2,1)S(1)} %dynamic-update-slic, ...), channel_id=1, replica_groups=mesh['wide'=16,'narrow'=2] {'wide','narrow'}, use_global_device_ids=true, to_apply=%add.1 | all-reduce | flops 7168 | bytes 28672
  58.7 58.7 %all-gather.2 = bf16[32,1,128]{2,1,0:T(2,128)(2,1)S(1)} all-gather(bf16[1,1,128]{2,1,0:T(2,128)(2,1)} %bitcast.217), channel_id=1, replica_groups=mesh['wide'=16,'narrow'=2] {'wide','narrow'}, dimensions={0}, use_global_device_ids=true | all-gather | bytes 8448 | tf_op jit(solution)/shard_map/all_gather | solution.py:196
  117.5 63.4 %all-gather.1 = bf16[32,32,3]{1,2,0:T(4,128)(2,1)S(1)} all-gather(bf16[1,32,3]{1,2,0:T(4,128)(2,1)} %bitcast.215), channel_id=1, replica_groups=mesh['wide'=16,'narrow'=2] {'wide','narrow'}, dimensions={0}, use_global_device_ids=true | all-gather | bytes 6336 | tf_op jit(solution)/shard_map/all_gather | solution.py:161
  181.0 66.1 %all-gather = bf16[32,32,3]{1,2,0:T(4,128)(2,1)S(1)} all-gather(bf16[1,32,3]{1,2,0:T(4,128)(2,1)} %bitcast.216), channel_id=1, replica_groups=mesh['wide'=16,'narrow'=2] {'wide','narrow'}, dimensions={0}, use_global_device_ids=true | all-gather | bytes 6336 | tf_op jit(solution)/shard_map/all_gather | solution.py:133
  250.7 12.2 fusion.15
  265.5 3.3 fusion.4
  268.9 11.6 reshape.318
  280.5 10.3 copy.157
  290.8 4.6 fusion.104
  308.1 3.2 fusion.37
  316.5 11.8 reshape.320
  328.3 10.0 copy.156
  338.3 4.8 select_reduce_fusion
  343.2 3.7 fusion
  349.1 5.9 fusion.49
  360.4 8.1 convolution_add_fusion
  368.6 58.6 %all-gather.20.cloned.1.call-done = bf16[4096,1024]{1,0:T(8,128)(2,1)} async-done(((bf16[128,1024]{1,0:T(8,128)(2,1)}), bf16[4096,1024]{1,0:T(8,128)(2,1)}) %all-gather.20.cloned.1.call-update) | async-done | bytes 8388624 | tf_op jit(solution)/shard_map/all_gather | solution.py:197
  427.2 7.4 fusion.103
  437.7 7.2 convert_reduce_fusion.1
  455.8 13.1 multiply_reduce_fusion
  468.9 12.4 multiply_convert_fusion
  481.4 3.1 convert_reduce_fusion.5
  485.2 3.0 multiply_reduce_fusion.3
  499.3 9.1 convert_bitcast_fusion
  512.5 6.5 copy.179
  519.1 3.4 copy.217
  528.1 3.8 fusion.73
  532.0 3.7 fusion.70
  541.9 6.4 convolution_bitcast_fusion
  548.2 12.6 copy.186
  560.9 4.9 convert_bitcast_fusion.1
  565.7 6.3 copy.177
  572.1 3.6 copy.216
  584.5 11.4 convolution_bitcast_fusion.1
  596.0 11.9 pad_maximum_fusion
  607.9 12.6 copy.190
  621.7 9.8 fusion.93
  632.7 10.3 fusion.86
  643.8 41.1 %all-reduce.15 = (f32[1024]{0:T(1024)S(1)}, f32[1024]{0:T(1024)S(1)}, f32[1024]{0:T(1024)S(1)}, f32[1024]{0:T(1024)S(1)}, f32[4096]{0:T(1024)S(1)}, /*index=5*/f...) all-reduce(f32[1024]{0:T(1024)S(1)} %get-tuple-element.97, ...), channel_id=5, replica_groups=mesh['wide'=16,'narrow'=2] {'wide','narrow'}, use_global_device_ids=true, to_apply=%region_25.26.clone | all-reduce | flops 11264 | bytes 90112
  689.6 5.9 fusion.41
  695.5 13.9 convolution_convert_fusion
  710.7 71.1 %reduce-scatter.31.cloned.1.call-done = f32[32,3]{1,0:T(8,128)} async-done(((f32[1024,3]{1,0:T(8,128)}), f32[32,3]{1,0:T(8,128)}) %reduce-scatter.31.cloned.1.call-update) | async-done | bytes 400
  783.3 140.7 %reduce-scatter.17.cloned.1.call-done = f32[32,1024]{1,0:T(8,128)} async-done(((f32[1024,1024]{1,0:T(8,128)}), f32[32,1024]{1,0:T(8,128)}) %reduce-scatter.17.cloned.1.call-update) | async-done | bytes 131088 | tf_op jit(solution)/shard_map/reduce_scatter | solution.py:325
  924.0 141.5 %reduce-scatter.19.cloned.1.call-done = f32[32,1024]{1,0:T(8,128)} async-done(((f32[1024,1024]{1,0:T(8,128)}), f32[32,1024]{1,0:T(8,128)}) %reduce-scatter.19.cloned.1.call-update) | async-done | bytes 131088 | tf_op jit(solution)/shard_map/reduce_scatter | solution.py:280
  1065.5 164.8 %reduce-scatter.25.cloned.1.call-done = f32[32,3072]{1,0:T(8,128)} async-done(((f32[1024,3072]{1,0:T(8,128)}), f32[32,3072]{1,0:T(8,128)}) %reduce-scatter.25.cloned.1.call-update) | async-done | bytes 393232
  1230.3 162.3 %reduce-scatter.29.cloned.1.call-done = f32[32,3072]{1,0:T(8,128)} async-done(((f32[1024,3072]{1,0:T(8,128)}), f32[32,3072]{1,0:T(8,128)}) %reduce-scatter.29.cloned.1.call-update) | async-done | bytes 393232
  1392.6 359.4 %reduce-scatter.21.cloned.1.call-done = f32[32,4096]{1,0:T(8,128)} async-done(((f32[1024,4096]{1,0:T(8,128)}), f32[32,4096]{1,0:T(8,128)}) %reduce-scatter.21.cloned.1.call-update) | async-done | bytes 524304 | tf_op jit(solution)/shard_map/reduce_scatter | solution.py:236
  1752.0 361.4 %reduce-scatter.23.cloned.1.call-done = f32[128,1024]{1,0:T(8,128)} async-done(((f32[4096,1024]{1,0:T(8,128)}), f32[128,1024]{1,0:T(8,128)}) %reduce-scatter.23.cloned.1.call-update) | async-done | bytes 524304 | tf_op jit(solution)/shard_map/reduce_scatter | solution.py:238
  (230 shorter events, 102.7 us)
Async XLA Ops:
  7.2 243.5 %all-gather.14.cloned.1.call-start = ((), (), s32[]{:S(2)}) async-start(), calls=%async_computation.10 | async-start | bytes 6488064 | tf_op jit(solution)/shard_map/all_gather | solution.py:159
  7.9 282.9 %all-gather.10.cloned.1.call-start = ((), (), s32[]{:S(2)}) async-start(), calls=%async_computation.8 | async-start | bytes 6488064 | tf_op jit(solution)/shard_map/all_gather | solution.py:131
  8.7 296.4 %all-gather.12.cloned.1.call-start = ((), (), s32[]{:S(2)}) async-start(), calls=%async_computation.9 | async-start | bytes 2162688 | tf_op jit(solution)/shard_map/all_gather | solution.py:132
  9.4 347.0 %all-gather.16.cloned.1.call-start = ((), (), s32[]{:S(2)}) async-start(), calls=%async_computation.11 | async-start | bytes 2162688 | tf_op jit(solution)/shard_map/all_gather | solution.py:160
  10.0 350.4 %all-gather.18.cloned.1.call-start = ((), (), s32[]{:S(2)}) async-start(), calls=%async_computation.12 | async-start | bytes 8650752 | tf_op jit(solution)/shard_map/all_gather | solution.py:195
  10.6 416.6 %all-gather.20.cloned.1.call-start = ((), (), s32[]{:S(2)}) async-start(), calls=%async_computation.13 | async-start | bytes 8650752 | tf_op jit(solution)/shard_map/all_gather | solution.py:197
  11.1 698.2 %reduce-scatter.27.cloned.1.call-start = ((), (), s32[]{:S(2)}) async-start(), calls=%async_computation.19 | async-start | bytes 540672
  280.5 10.3 copy-start.29
  299.5 2.5 copy-start.18
  301.1 2.7 copy-start.19
  343.2 6.0 copy-start
  427.2 7.6 copy-start.24
  434.5 3.2 copy-start.16
  435.9 9.0 slice-start
  437.7 7.2 copy-start.26
  437.7 7.2 copy-start.5
  437.7 7.2 slice-start.1
  444.9 2.8 copy-start.34
  444.9 4.1 copy-start.15
  468.9 12.4 copy-start.3
  481.4 3.2 copy-start.1
  481.4 3.8 copy-start.10
  485.1 3.4 copy-start.32
  485.1 4.4 copy-start.14
  496.3 2.0 copy-start.25
  496.3 2.9 copy-start.17
  509.4 1.8 copy-start.12
  519.1 3.4 copy-start.21
  519.1 3.6 copy-start.23
  522.5 5.6 copy-start.8
  524.0 257.9 %reduce-scatter.31.cloned.1.call-start = ((), (), s32[]{:S(2)}) async-start(), calls=%async_computation.21 | async-start | bytes 540672
  528.0 4.0 copy-start.11
  528.0 395.9 %reduce-scatter.17.cloned.1.call-start = ((), (), s32[]{:S(2)}) async-start(), calls=%async_computation.14 | async-start | bytes 4325376 | tf_op jit(solution)/shard_map/reduce_scatter | solution.py:325
  531.9 533.6 %reduce-scatter.19.cloned.1.call-start = ((), (), s32[]{:S(2)}) async-start(), calls=%async_computation.15 | async-start | bytes 4325376 | tf_op jit(solution)/shard_map/reduce_scatter | solution.py:280
  535.7 1.2 copy-start.13
  535.7 694.6 %reduce-scatter.25.cloned.1.call-start = ((), (), s32[]{:S(2)}) async-start(), calls=%async_computation.18 | async-start | bytes 12976128
  536.9 3.7 copy-start.22
  536.9 5.0 copy-start.30
  540.7 1.2 copy-start.28
  560.8 831.8 %reduce-scatter.29.cloned.1.call-start = ((), (), s32[]{:S(2)}) async-start(), calls=%async_computation.20 | async-start | bytes 12976128
  575.7 2.2 copy-start.2
  577.9 1.0 copy-start.33
  579.0 5.6 copy-start.31
  579.0 5.6 copy-start.39
  620.5 1.2 copy-start.6
  620.5 1131.5 %reduce-scatter.21.cloned.1.call-start = ((), (), s32[]{:S(2)}) async-start(), calls=%async_computation.16 | async-start | bytes 17301504 | tf_op jit(solution)/shard_map/reduce_scatter | solution.py:236
  631.5 1.2 copy-start.27
  631.5 1481.9 %reduce-scatter.23.cloned.1.call-start = ((), (), s32[]{:S(2)}) async-start(), calls=%async_computation.17 | async-start | bytes 17301504 | tf_op jit(solution)/shard_map/reduce_scatter | solution.py:238
  (8 other events, 6.8 us)
Sparse Core Ops, SparseCore 0:
  10.9 71.0 all-gather.13
  84.9 68.1 all-gather.9
  156.1 55.0 all-gather.11
  214.0 55.3 all-gather.15
  272.3 76.1 all-gather.17
  351.3 75.8 all-gather.19
  524.1 125.4 reduce-scatter.26
  652.0 129.8 reduce-scatter.30
  784.7 139.1 reduce-scatter.16
  926.7 138.7 reduce-scatter.18
  1072.1 158.1 reduce-scatter.24
  1237.8 154.7 reduce-scatter.28
  1395.5 356.4 reduce-scatter.20
  1754.7 358.6 reduce-scatter.22
where the time goes:
time: 2130 us; the launch traced here: 2120 us
  waiting for transfers between devices  1460 us (69%)
  blocking collectives  271 us (13%)
  matrix products  173 us (8%)
  local copies, waits for them, and re-layouts  153 us (7%)
  other arithmetic  43.8 us (2%)
    unnamed x18, waiting for transfers between devices  402 us
    reduce_scatter x1, waiting for transfers between devices, shards(): lax.psum_scatter(down_grad, ('wide', 'narrow'), scatter_dimension=0, tile...  361 us
    reduce_scatter x1, waiting for transfers between devices, shards(): lax.psum_scatter(up_grad, ('wide', 'narrow'), scatter_dimension=0, tiled=...  359 us
    reduce_scatter x1, waiting for transfers between devices, shards(): lax.psum_scatter(cross_proj_grad, ('wide', 'narrow'), scatter_dimension=0...  142 us
    reduce_scatter x1, waiting for transfers between devices, shards(): lax.psum_scatter(self_out_part, ('wide', 'narrow'), scatter_dimension=0,...  141 us
    unnamed x2, blocking collectives  82.8 us
    all_gather x1, blocking collectives, shards(): lax.all_gather(self_bias, ('wide', 'narrow'), axis=1, tiled=True)  66.1 us
    unnamed x117, local copies, waits for them, and re-layouts  65 us
  transfers between devices with their start and end apart: 14, of which 8 were waited for; matrix products, arithmetic and copies ran while one was open for 12% of the time, Pallas kernels for 0%

commit v1 on v0

--- a/solution.py
+++ b/solution.py
@@ -1,9 +1,398 @@
+import functools
 import math
 
 import jax
 import jax.numpy as jnp
 from jax import lax
+from jax.experimental import pallas as pl
+from jax.experimental.pallas import tpu as pltpu
 from jax.sharding import PartitionSpec as P
+
+MESH = pl.DeviceIdType.MESH
+AXES = ("wide", "narrow")
+LANE_CHUNK = 1024
+
+
+def places(far_count):
+    wide = lax.axis_index("wide")
+    x = lax.axis_index("narrow")
+    far = wide // 4
+    y = (wide // 2) % 2
+    core = wide % 2
+    near_y = y + core * (1 - 2 * y)
+    near_x = x + (1 - core) * (1 - 2 * x)
+    other_y = y + (1 - core) * (1 - 2 * y)
+    other_x = x + core * (1 - 2 * x)
+
+    def device(f, yy, cc, xx):
+        return (f * 4 + yy * 2 + cc, xx)
+
+    return dict(
+        far=far,
+        y=y,
+        core=core,
+        x=x,
+        near=(near_y, near_x),
+        other=(other_y, other_x),
+        diagonal=(1 - y, 1 - x),
+        near_device=device(far, near_y, core, near_x),
+        other_device=device(far, other_y, core, other_x),
+        twin_device=device(far, y, 1 - core, x),
+        far_devices=[
+            (lax.rem(far + d, far_count), device(lax.rem(far + d, far_count), y, core, x))
+            for d in range(1, far_count)
+        ],
+    )
+
+
+def greet(where):
+    barrier = pltpu.get_barrier_semaphore()
+    partners = [where["near_device"], where["other_device"], where["twin_device"]]
+    partners += [device for _, device in where["far_devices"]]
+    for device in partners:
+        pl.semaphore_signal(barrier, inc=1, device_id=device, device_id_type=MESH)
+    pl.semaphore_wait(barrier, len(partners))
+
+
+def remote(src, dst, send_sem, recv_sem, device):
+    return pltpu.make_async_remote_copy(
+        src_ref=src,
+        dst_ref=dst,
+        send_sem=send_sem,
+        recv_sem=recv_sem,
+        device_id=device,
+        device_id_type=MESH,
+    )
+
+
+def gather_kernel(far_count, chunks, n_arrays, skew, *refs):
+    ins, outs = refs[:n_arrays], refs[n_arrays : 2 * n_arrays]
+    local_sem, send_sem, recv_sem = refs[2 * n_arrays :]
+    me = places(far_count)
+    far, y, core, x = me["far"], me["y"], me["core"], me["x"]
+    far_all = pl.ds(0, far_count)
+
+    def block(ref, k, *lead):
+        _, row, rows, col, cols = chunks[k]
+        return ref.at[(*lead, pl.ds(row, rows), pl.ds(col, cols))]
+
+    def own(k):
+        return block(ins[chunks[k][0]], k)
+
+    def at(k, *lead):
+        return block(outs[chunks[k][0]], k, *lead)
+
+    local = []
+    for a in range(n_arrays):
+        copy = pltpu.make_async_copy(ins[a], outs[a].at[far, y, core, x], local_sem.at[a])
+        copy.start()
+        local.append(copy)
+    greet(me)
+
+    sent = []
+
+    def go(copy):
+        copy.start()
+        sent.append(copy)
+        return copy
+
+    far_copies, near_copies, other_copies, pass_copies, twin_copies = {}, {}, {}, {}, {}
+    lanes = far_count - 1
+
+    def start_far(k):
+        far_copies[k] = [
+            go(
+                remote(
+                    own(k),
+                    at(k, far, y, core, x),
+                    send_sem.at[k, d],
+                    recv_sem.at[k, d],
+                    device,
+                )
+            )
+            for d, (_, device) in enumerate(me["far_devices"])
+        ]
+
+    def start_near(k):
+        column = at(k, far_all, y, core, x)
+        near_copies[k] = go(
+            remote(column, column, send_sem.at[k, lanes], recv_sem.at[k, lanes], me["near_device"])
+        )
+        other_copies[k] = go(
+            remote(
+                column, column, send_sem.at[k, lanes + 1], recv_sem.at[k, lanes + 1], me["other_device"]
+            )
+        )
+
+    def start_pass(k):
+        column = at(k, far_all, me["near"][0], core, me["near"][1])
+        pass_copies[k] = go(
+            remote(
+                column, column, send_sem.at[k, lanes + 2], recv_sem.at[k, lanes + 2], me["other_device"]
+            )
+        )
+
+    def start_twin(k):
+        half = at(k, far_all, pl.ds(0, 2), core, pl.ds(0, 2))
+        twin_copies[k] = go(
+            remote(half, half, send_sem.at[k, lanes + 3], recv_sem.at[k, lanes + 3], me["twin_device"])
+        )
+
+    count = len(chunks)
+    for t in range(count + 3 * skew):
+        k = t - 3 * skew
+        if 0 <= k < count:
+            other_copies[k].wait_recv()
+            pass_copies[k].wait_recv()
+            start_twin(k)
+        k = t - 2 * skew
+        if 0 <= k < count:
+            near_copies[k].wait_recv()
+            start_pass(k)
+        k = t - skew
+        if 0 <= k < count:
+            if k == 0:
+                for copy in local:
+                    copy.wait()
+            for copy in far_copies[k]:
+                copy.wait_recv()
+            start_near(k)
+        if t < count:
+            start_far(t)
+    for k in range(count):
+        twin_copies[k].wait_recv()
+    for copy in sent:
+        copy.wait_send()
+
+
+def gather_all(mesh, shards, chunks, skew, collective_id):
+    far_count = mesh.shape["wide"] // 4
+    n = len(shards)
+    outs = [
+        jax.ShapeDtypeStruct((far_count, 2, 2, 2) + s.shape, s.dtype) for s in shards
+    ]
+    lanes = far_count + 3
+    return pl.pallas_call(
+        functools.partial(gather_kernel, far_count, chunks, n, skew),
+        out_shape=outs,
+        in_specs=[pl.BlockSpec(memory_space=pl.ANY)] * n,
+        out_specs=[pl.BlockSpec(memory_space=pl.ANY)] * n,
+        scratch_shapes=[
+            pltpu.SemaphoreType.DMA((n,)),
+            pltpu.SemaphoreType.DMA((len(chunks), lanes)),
+            pltpu.SemaphoreType.DMA((len(chunks), lanes)),
+        ],
+        compiler_params=pltpu.CompilerParams(collective_id=collective_id, has_side_effects=True),
+        name="gather_params",
+    )(*shards)
+
+
+def scatter_kernel(far_count, chunks, n_arrays, skew, *refs):
+    ins, outs = refs[:n_arrays], refs[n_arrays : 2 * n_arrays]
+    (mine, from_twin, from_other, from_near, from_far, mine_s, twin_s, other_s, near_s, far_s,
+     local_sem, send_sem, recv_sem) = refs[2 * n_arrays :]
+    me = places(far_count)
+    far, y, core, x = me["far"], me["y"], me["core"], me["x"]
+    far_all = pl.ds(0, far_count)
+    small = len(chunks) - 1
+    slots = mine.shape[0]
+
+    def buffers(k):
+        if k == small:
+            return mine_s, twin_s, other_s, near_s, far_s
+        return mine.at[k % slots], from_twin.at[k], from_other.at[k], from_near.at[k], from_far.at[k]
+
+    def half(k, c):
+        a, row, rows, col, cols = chunks[k]
+        return ins[a].at[far_all, pl.ds(0, 2), c, pl.ds(0, 2), pl.ds(row, rows), pl.ds(col, cols)]
+
+    sent, loads, twins, others, nears, fars = [], {}, {}, {}, {}, {}
+
+    def go(copy):
+        copy.start()
+        sent.append(copy)
+        return copy
+
+    def start_load(k):
+        loads[k] = pltpu.make_async_copy(half(k, core), buffers(k)[0], local_sem.at[k])
+        loads[k].start()
+
+    def start_twin(k):
+        twins[k] = go(
+            remote(half(k, 1 - core), buffers(k)[1], send_sem.at[k, 0], recv_sem.at[k, 0], me["twin_device"])
+        )
+
+    def add_mine(k):
+        own, total = buffers(k)[:2]
+
+        def body(i, carry):
+            f, yy, xx = i // 4, (i // 2) % 2, i % 2
+            total[f, yy, xx] = total[f, yy, xx] + own[f, yy, xx]
+            return carry
+
+        lax.fori_loop(0, far_count * 4, body, 0)
+
+    def start_other(k):
+        total, landing = buffers(k)[1:3]
+        others[k] = [
+            go(
+                remote(
+                    total.at[far_all, place[0], place[1]],
+                    landing.at[i],
+                    send_sem.at[k, 1 + i],
+                    recv_sem.at[k, 1 + i],
+                    me["other_device"],
+                )
+            )
+            for i, place in enumerate((me["diagonal"], me["other"]))
+        ]
+
+    def add_other(k, i):
+        total, landing = buffers(k)[1:3]
+        place = (me["near"], (y, x))[i]
+
+        def body(f, carry):
+            total[f, place[0], place[1]] = total[f, place[0], place[1]] + landing[i, f]
+            return carry
+
+        lax.fori_loop(0, far_count, body, 0)
+
+    def start_near(k):
+        _, total, _, landing, _ = buffers(k)
+        nears[k] = go(
+            remote(
+                total.at[far_all, me["near"][0], me["near"][1]],
+                landing,
+                send_sem.at[k, 3],
+                recv_sem.at[k, 3],
+                me["near_device"],
+            )
+        )
+
+    def add_near(k):
+        _, total, _, landing, _ = buffers(k)
+
+        def body(f, carry):
+            total[f, y, x] = total[f, y, x] + landing[f]
+            return carry
+
+        lax.fori_loop(0, far_count, body, 0)
+
+    def start_far(k):
+        _, total, _, _, landing = buffers(k)
+        fars[k] = [
+            go(
+                remote(
+                    total.at[target, y, x],
+                    landing.at[d],
+                    send_sem.at[k, 4 + d],
+                    recv_sem.at[k, 4 + d],
+                    device,
+                )
+            )
+            for d, (target, device) in enumerate(me["far_devices"])
+        ]
+
+    def finish(k):
+        _, total, _, _, landing = buffers(k)
+        a, row, rows, col, cols = chunks[k]
+        result = total[far, y, x].astype(jnp.float32)
+        for d in range(far_count - 1):
+            result += landing[d].astype(jnp.float32)
+        outs[a][pl.ds(row, rows), pl.ds(col, cols)] = result
+
+    count = len(chunks)
+    start_load(0)
+    greet(me)
+    for t in range(count + 4 * skew):
+        k = t - 4 * skew
+        if 0 <= k < count:
+            for copy in fars[k]:
+                copy.wait_recv()
+            finish(k)
+        k = t - 3 * skew
+        if 0 <= k < count:
+            nears[k].wait_recv()
+            add_near(k)
+            start_far(k)
+        k = t - 2 * skew
+        if 0 <= k < count:
+            others[k][0].wait_recv()
+            add_other(k, 0)
+            start_near(k)
+            others[k][1].wait_recv()
+            add_other(k, 1)
+        k = t - skew
+        if 0 <= k < count:
+            loads[k].wait()
+            twins[k].wait_recv()
+            add_mine(k)
+            start_other(k)
+        if t < count:
+            start_twin(t)
+            if t + 1 < count:
+                start_load(t + 1)
+    for copy in sent:
+        copy.wait_send()
+
+
+def scatter_all(mesh, grads, chunks, skew, collective_id):
+    far_count = mesh.shape["wide"] // 4
+    n = len(grads)
+    main = len(chunks) - 1
+    rows, cols = chunks[0][2], chunks[0][4]
+    small_shape = grads[-1].shape[4:]
+    low = grads[0].dtype
+    slots = skew + 2
+    lanes = far_count + 3
+    return pl.pallas_call(
+        functools.partial(scatter_kernel, far_count, chunks, n, skew),
+        out_shape=[jax.ShapeDtypeStruct(g.shape[4:], jnp.float32) for g in grads],
+        in_specs=[pl.BlockSpec(memory_space=pl.ANY)] * n,
+        out_specs=[pl.BlockSpec(memory_space=pltpu.VMEM)] * n,
+        scratch_shapes=[
+            pltpu.VMEM((slots, far_count, 2, 2, rows, cols), low),
+            pltpu.VMEM((main, far_count, 2, 2, rows, cols), low),
+            pltpu.VMEM((main, 2, far_count, rows, cols), low),
+            pltpu.VMEM((main, far_count, rows, cols), low),
+            pltpu.VMEM((main, far_count - 1, rows, cols), low),
+            pltpu.VMEM((far_count, 2, 2) + small_shape, jnp.float32),
+            pltpu.VMEM((far_count, 2, 2) + small_shape, jnp.float32),
+            pltpu.VMEM((2, far_count) + small_shape, jnp.float32),
+            pltpu.VMEM((far_count,) + small_shape, jnp.float32),
+            pltpu.VMEM((far_count - 1,) + small_shape, jnp.float32),
+            pltpu.SemaphoreType.DMA((main + 1,)),
+            pltpu.SemaphoreType.DMA((main + 1, lanes)),
+            pltpu.SemaphoreType.DMA((main + 1, lanes)),
+        ],
+        compiler_params=pltpu.CompilerParams(
+            collective_id=collective_id, has_side_effects=True, vmem_limit_bytes=60 * 2**20
+        ),
+        name="scatter_grads",
+    )(*grads)
+
+
+def chunk_list(shapes):
+    rows = shapes[0][0]
+    chunks = []
+    for a, (all_rows, all_cols) in enumerate(shapes[:-1]):
+        for row in range(0, all_rows, rows):
+            for col in range(0, all_cols, LANE_CHUNK):
+                chunks.append((a, row, rows, col, LANE_CHUNK))
+    last = shapes[-1]
+    chunks.append((len(shapes) - 1, 0, last[0], 0, last[1]))
+    return chunks
+
+GATHER_SKEW = 1
+SCATTER_SKEW = 1
+
+
+def small_widths(per_device, up_rows):
+    return [
+        3 * per_device, per_device, per_device, 3 * per_device, per_device, per_device,
+        up_rows, per_device, per_device, per_device,
+    ]
+
 
 H = 16
 HD = 64
@@ -91,6 +480,7 @@
 
 
 def shards(
+    mesh,
     target_input,
     memory,
     cotangent,
@@ -127,14 +517,31 @@
         positions[None, None, :] < tgt_lengths[:, None, None]
     )
     cross_usable = jnp.arange(mem_len)[None, None, :] < mem_lengths[:, None, None]
-    self_whole = (
-        lax.all_gather(self_qkv, ("wide", "narrow"), axis=0, tiled=True),
-        lax.all_gather(self_out, ("wide", "narrow"), axis=0, tiled=True),
-        lax.all_gather(self_bias, ("wide", "narrow"), axis=1, tiled=True),
-        lax.all_gather(norm1_gain, ("wide", "narrow"), axis=0, tiled=True),
-        lax.all_gather(norm1_shift, ("wide", "narrow"), axis=0, tiled=True),
-    )
-    qkv_weight, out_weight, self_rows, gain_one, shift_one = self_whole
+    widths = small_widths(model_width // mesh.size, up_bias.shape[0])
+    smalls = [
+        self_bias, norm1_gain, norm1_shift, cross_bias, norm2_gain, norm2_shift,
+        up_bias, down_bias, norm3_gain, norm3_shift,
+    ]
+    small = jnp.concatenate([v.reshape(-1) for v in smalls])
+    small = jnp.pad(small, (0, 2048 - small.shape[0])).reshape(16, 128)
+    arrays = [self_qkv, self_out, cross_qkv, cross_out, ffn_up, ffn_down, small]
+    chunks = chunk_list([v.shape for v in arrays])
+    gathered = gather_all(mesh, arrays, chunks[-1:] + chunks[:-1], GATHER_SKEW, 0)
+    qkv_weight, out_weight, cross_in, cross_proj, up_weight, down_weight = [
+        v.reshape(-1, v.shape[-1]) for v in gathered[:-1]
+    ]
+    small_all = gathered[-1].reshape(mesh.size, 2048)
+    taken, at = [], 0
+    for v, width in zip(smalls, widths):
+        part = small_all[:, at : at + width]
+        if v.ndim == 2:
+            part = part.reshape(mesh.size, 3, width // 3).transpose(1, 0, 2).reshape(3, -1)
+        else:
+            part = part.reshape(-1)
+        taken.append(part)
+        at += width
+    (self_rows, gain_one, shift_one, cross_rows, gain_two, shift_two,
+     up_shift, down_shift, gain_three, shift_three) = taken
     self_shift = self_rows.astype(jnp.float32)
     projected = jnp.dot(inputs_flat, qkv_weight, preferred_element_type=jnp.float32)
     self_q = (
@@ -155,14 +562,6 @@
         shift_one.astype(jnp.float32),
     )
     hidden_one_low = hidden_one.astype(jnp.bfloat16)
-    cross_whole = (
-        lax.all_gather(cross_qkv, ("wide", "narrow"), axis=0, tiled=True),
-        lax.all_gather(cross_out, ("wide", "narrow"), axis=0, tiled=True),
-        lax.all_gather(cross_bias, ("wide", "narrow"), axis=1, tiled=True),
-        lax.all_gather(norm2_gain, ("wide", "narrow"), axis=0, tiled=True),
-        lax.all_gather(norm2_shift, ("wide", "narrow"), axis=0, tiled=True),
-    )
-    cross_in, cross_proj, cross_rows, gain_two, shift_two = cross_whole
     cross_shift = cross_rows.astype(jnp.float32)
     cross_q = (
         (
@@ -191,15 +590,6 @@
         hidden_one + cross_branch, gain_two.astype(jnp.float32), shift_two.astype(jnp.float32)
     )
     hidden_two_low = hidden_two.astype(jnp.bfloat16)
-    ffn_whole = (
-        lax.all_gather(ffn_up, ("wide", "narrow"), axis=0, tiled=True),
-        lax.all_gather(up_bias, ("wide", "narrow"), axis=0, tiled=True),
-        lax.all_gather(ffn_down, ("wide", "narrow"), axis=0, tiled=True),
-        lax.all_gather(down_bias, ("wide", "narrow"), axis=0, tiled=True),
-        lax.all_gather(norm3_gain, ("wide", "narrow"), axis=0, tiled=True),
-        lax.all_gather(norm3_shift, ("wide", "narrow"), axis=0, tiled=True),
-    )
-    up_weight, up_shift, down_weight, down_shift, gain_three, shift_three = ffn_whole
     pre_act = jnp.dot(
         hidden_two_low, up_weight, preferred_element_type=jnp.float32
     ) + up_shift.astype(jnp.float32)
@@ -212,15 +602,6 @@
         hidden_two + ffn_branch, gain_three.astype(jnp.float32), shift_three.astype(jnp.float32)
     )
     block_out = result.astype(jnp.bfloat16).reshape(samples_dev, tgt_len, model_width)
-    ffn_back = (
-        lax.all_gather(ffn_up, ("wide", "narrow"), axis=0, tiled=True),
-        lax.all_gather(up_bias, ("wide", "narrow"), axis=0, tiled=True),
-        lax.all_gather(ffn_down, ("wide", "narrow"), axis=0, tiled=True),
-        lax.all_gather(down_bias, ("wide", "narrow"), axis=0, tiled=True),
-        lax.all_gather(norm3_gain, ("wide", "narrow"), axis=0, tiled=True),
-        lax.all_gather(norm3_shift, ("wide", "narrow"), axis=0, tiled=True),
-    )
-    up_weight, up_shift, down_weight, down_shift, gain_three, shift_three = ffn_back
     upstream = cotangent.reshape(tgt_rows, model_width).astype(jnp.float32)
     d_sum3, gain3_grad, shift3_grad = norm_backward(
         upstream, normed_three, inverse_three, gain_three.astype(jnp.float32)
@@ -232,22 +613,6 @@
     up_grad = column_products(hidden_two_low, d_pre)
     up_shift_grad = row_sums(d_pre)
     d_hidden2 = d_sum3 + times_transpose(d_pre, up_weight)
-    ffn_parts = (
-        lax.psum_scatter(up_grad, ("wide", "narrow"), scatter_dimension=0, tiled=True),
-        lax.psum_scatter(up_shift_grad, ("wide", "narrow"), scatter_dimension=0, tiled=True),
-        lax.psum_scatter(down_grad, ("wide", "narrow"), scatter_dimension=0, tiled=True),
-        lax.psum_scatter(down_shift_grad, ("wide", "narrow"), scatter_dimension=0, tiled=True),
-        lax.psum_scatter(gain3_grad, ("wide", "narrow"), scatter_dimension=0, tiled=True),
-        lax.psum_scatter(shift3_grad, ("wide", "narrow"), scatter_dimension=0, tiled=True),
-    )
-    cross_back = (
-        lax.all_gather(cross_qkv, ("wide", "narrow"), axis=0, tiled=True),
-        lax.all_gather(cross_out, ("wide", "narrow"), axis=0, tiled=True),
-        lax.all_gather(cross_bias, ("wide", "narrow"), axis=1, tiled=True),
-        lax.all_gather(norm2_gain, ("wide", "narrow"), axis=0, tiled=True),
-        lax.all_gather(norm2_shift, ("wide", "narrow"), axis=0, tiled=True),
-    )
-    cross_in, cross_proj, cross_rows, gain_two, shift_two = cross_back
     d_sum2, gain2_grad, shift2_grad = norm_backward(
         d_hidden2, normed_two, inverse_two, gain_two.astype(jnp.float32)
     )
@@ -275,21 +640,6 @@
         .reshape(samples_dev, mem_len, model_width)
     )
     d_hidden1 = d_sum2 + times_transpose(d_cross_q, cross_in[:, :model_width])
-    cross_parts = (
-        lax.psum_scatter(cross_in_grad, ("wide", "narrow"), scatter_dimension=0, tiled=True),
-        lax.psum_scatter(cross_proj_grad, ("wide", "narrow"), scatter_dimension=0, tiled=True),
-        lax.psum_scatter(cross_shift_grad, ("wide", "narrow"), scatter_dimension=1, tiled=True),
-        lax.psum_scatter(gain2_grad, ("wide", "narrow"), scatter_dimension=0, tiled=True),
-        lax.psum_scatter(shift2_grad, ("wide", "narrow"), scatter_dimension=0, tiled=True),
-    )
-    self_back = (
-        lax.all_gather(self_qkv, ("wide", "narrow"), axis=0, tiled=True),
-        lax.all_gather(self_out, ("wide", "narrow"), axis=0, tiled=True),
-        lax.all_gather(self_bias, ("wide", "narrow"), axis=1, tiled=True),
-        lax.all_gather(norm1_gain, ("wide", "narrow"), axis=0, tiled=True),
-        lax.all_gather(norm1_shift, ("wide", "narrow"), axis=0, tiled=True),
-    )
-    qkv_weight, out_weight, self_rows, gain_one, shift_one = self_back
     d_sum1, gain1_grad, shift1_grad = norm_backward(
         d_hidden1, normed_one, inverse_one, gain_one.astype(jnp.float32)
     )
@@ -320,39 +670,41 @@
         .astype(jnp.bfloat16)
         .reshape(samples_dev, tgt_len, model_width)
     )
-    self_parts = (
-        lax.psum_scatter(self_qkv_part, ("wide", "narrow"), scatter_dimension=0, tiled=True),
-        lax.psum_scatter(self_out_part, ("wide", "narrow"), scatter_dimension=0, tiled=True),
-        lax.psum_scatter(self_shift_grad, ("wide", "narrow"), scatter_dimension=1, tiled=True),
-        lax.psum_scatter(gain1_grad, ("wide", "narrow"), scatter_dimension=0, tiled=True),
-        lax.psum_scatter(shift1_grad, ("wide", "narrow"), scatter_dimension=0, tiled=True),
-    )
+    grads = [self_qkv_part, self_out_part, cross_in_grad, cross_proj_grad, up_grad, down_grad]
+    sums = [
+        self_shift_grad, gain1_grad, shift1_grad, cross_shift_grad, gain2_grad, shift2_grad,
+        up_shift_grad, down_shift_grad, gain3_grad, shift3_grad,
+    ]
+    parts = []
+    for v in sums:
+        if v.ndim == 2:
+            v = v.reshape(3, mesh.size, -1).transpose(1, 0, 2)
+        parts.append(v.reshape(mesh.size, -1))
+    packed = jnp.concatenate(parts, axis=1)
+    packed = jnp.pad(packed, ((0, 0), (0, 1024 - packed.shape[1])))
+    lead = (mesh.shape["wide"] // 4, 2, 2, 2)
+    stacked = [
+        g.astype(jnp.bfloat16).reshape(lead + (-1, g.shape[-1])) for g in grads
+    ] + [packed.reshape(lead + (8, 128))]
+    chunks = chunk_list([g.shape[4:] for g in stacked])
+    reduced = scatter_all(mesh, stacked, chunks, SCATTER_SKEW, 1)
+    small_sums = reduced[-1].reshape(-1)
+    outs, at = [], 0
+    for v, width in zip(sums, widths):
+        part = small_sums[at : at + width]
+        outs.append(part.reshape(3, -1) if v.ndim == 2 else part)
+        at += width
     return (
-        block_out,
-        target_grad,
-        memory_grad,
-        self_parts[0],
-        self_parts[1],
-        self_parts[2],
-        self_parts[3],
-        self_parts[4],
-        cross_parts[0],
-        cross_parts[1],
-        cross_parts[2],
-        cross_parts[3],
-        cross_parts[4],
-        ffn_parts[0],
-        ffn_parts[1],
-        ffn_parts[2],
-        ffn_parts[3],
-        ffn_parts[4],
-        ffn_parts[5],
+        block_out, target_grad, memory_grad,
+        reduced[0], reduced[1], outs[0], outs[1], outs[2],
+        reduced[2], reduced[3], outs[3], outs[4], outs[5],
+        reduced[4], outs[6], reduced[5], outs[7], outs[8], outs[9],
     )
 
 
 def solution(mesh):
     return jax.shard_map(
-        shards,
+        functools.partial(shards, mesh),
         mesh=mesh,
         in_specs=(
             P(("wide", "narrow"), None, None),

time: 2130 us -> 698 us (0.33)
  waiting for transfers between devices: 1460 us -> 0 us
  Pallas kernels: 0 us -> 388 us
  blocking collectives: 271 us -> 0 us
  local copies, waits for them, and re-layouts: 153 us -> 99.5 us
    reduce_scatter x4 -> x0, waiting for transfers between devices: 1000 us -> none  [the longest x1 361 us: shards(): lax.psum_scatter(down_grad, ('wide', 'narrow'), scatter_dimension=0, tile...]
    unnamed x18 -> x0, waiting for transfers between devices: 402 us -> none
    pallas_call x0 -> x2, Pallas kernels: none -> 388 us  [the longest x1 201 us: scatter_all(): pl.pallas_call(functools.partial(scatter_kernel, far_count, chunks, n, sk...]
    all_gather x3 -> x0, blocking collectives: 188 us -> none  [the longest x1 66.1 us: shards(): lax.all_gather(self_bias, ('wide', 'narrow'), axis=1, tiled=True)]
    unnamed x2 -> x0, blocking collectives: 82.8 us -> none
    all_gather x6 -> x0, waiting for transfers between devices: 58.7 us -> none  [the longest x1 58.6 us: shards(): lax.all_gather(ffn_down, ('wide', 'narrow'), axis=0, tiled=True)]
    unnamed x117 -> x128, local copies, waits for them, and re-layouts: 65 us -> 35.7 us
  transfers between devices with their start and end apart: 14 -> 0, of which waited for: 8 -> 0; matrix products, arithmetic and copies ran while one was open for 12% -> 0% of each run, Pallas kernels for 0% -> 0%
where the time goes in v1:
time: 698 us; the launch traced here: 690 us
  Pallas kernels  388 us (56%)
  matrix products  155 us (22%)
  local copies, waits for them, and re-layouts  99.5 us (14%)
  other arithmetic  45.2 us (6%)
    pallas_call x1, Pallas kernels, scatter_all(): pl.pallas_call(functools.partial(scatter_kernel, far_count, chunks, n, sk...  201 us
    pallas_call x1, Pallas kernels, gather_all(): pl.pallas_call(functools.partial(gather_kernel, far_count, chunks, n, ske...  187 us
    unnamed x128, local copies, waits for them, and re-layouts  35.7 us
    dot_general x7, matrix products, times_transpose(): lax.dot_general(left_side, right_side, (((1,), (1,)), ((), ())), preferre...  35 us
    dot_general x7, matrix products, column_products(): lax.dot_general(left_side, right_side, (((0,), (0,)), ((), ())), preferre...  32.3 us
    dot_general x2, matrix products, attend_back(): jnp.einsum('sqhe,skhe->shqk', upstream, values, preferred_element_type=jn...  14.1 us

profile of v1, /device:TPU:4, one launch (start us, length us, event | category | flops | bytes accessed | tf_op | source)
XLA Modules:
  0.0 690.5 jit_solution(4379154526257672694)
XLA Ops:
  2.2 5.4 concatenate.23
  8.2 186.9 %gather_params.1 = (bf16[4,2,2,2,32,3072]{5,4,3,2,1,0:T(8,128)(2,1)}, bf16[4,2,2,2,32,1024]{5,4,3,2,1,0:T(8,128)(2,1)}, bf16[4,2,2,2,32,3072]{5,4,3,2,1,0:T(8,12...) custom-call(bf16[32,3072]{1,0:T(8,128)(2,1)} %refs_0_.1, ...), custom_call_target="tpu_custom_call" | custom-call | tf_op jit(solution)/shard_map/gather_params/pallas_call | solution.py:175
  197.6 12.3 %convolution_bitcast_fusion = f32[2048,2048]{0,1:T(8,128)S(1)} fusion(bf16[2048,1024]{1,0:T(8,128)(2,1)} %bitcast.250, bf16[1024,3072]{1,0:T(8,128)(2,1)} %bitcast.225), kind=kOutput, calls=%fused_computation.8 | convolution fusion | flops 8589934592 | bytes 25165824 | tf_op jit(solution)/shard_map/dot_general | solution.py:579
  209.9 5.7 copy-done.12
  215.6 2.7 slice.222
  218.3 8.0 %reshape.465 = bf16[2,1024,16,64]{1,0,3,2:T(2,128)(2,1)} reshape(bf16[2048,1024]{0,1:T(8,128)(2,1)} %slice.222) | data formatting | bytes 8388608 | tf_op jit(solution)/shard_map/reshape | solution.py:580
  226.7 4.7 convolution_bitcast_fusion.1
  233.4 2.7 fusion.70
  241.6 3.5 fusion.49
  245.0 2.0 reshape.464
  247.0 5.3 select_reduce_fusion
  252.4 3.5 fusion
  255.9 2.2 copy-done
  258.1 5.9 fusion.4
  264.0 7.8 %reshape.463 = bf16[2,1024,16,64]{1,0,3,2:T(2,128)(2,1)} reshape(bf16[2048,1024]{0,1:T(8,128)(2,1)} %fusion.4) | data formatting | bytes 8388608 | tf_op jit(solution)/shard_map/reshape | solution.py:582
  271.8 10.0 %fusion.64 = bf16[2,128,16,64]{1,3,2,0:T(8,128)(2,1)S(1)} fusion(f32[2,16,128,1024]{3,2,1,0:T(8,128)} %copy-done, f32[2,16,128]{2,1,0:T(8,128)S(1)} %fusion, f32[2,16,128]{2,1,0:T(8,128)S(1)} %get-tuple-element.97, pred[2,1024]{1,0:T(4,128)(4,1)S(1)} %iota_compare_fusion.1, bf16[2,1024,16,64]{1,0,3,2:T(2,128)(2,1)} %reshape.463), kind=kOutput, calls=%fused_computation.90 | convolution fusion | flops 553910272 | bytes 21530624 | tf_op jit(solution)/shard_map/shqk,skhe->sqhe/dot_general | solution.py:458
  285.8 7.1 %multiply_convert_fusion.1 = (bf16[256,4096]{1,0:T(8,128)(2,1)S(1)}, f32[256,4096]{1,0:T(8,128)}) fusion(f32[4096]{0:T(1024)S(1)} %fusion.105, bf16[1024,4096]{1,0:T(8,128)(2,1)} %bitcast.242, f32[256,1024]{1,0:T(8,128)} %get-tuple-element.100, f32[1024]{0:T(1024)S(1)} %reshape.500, f32[1024]{0:T(1024)S(1)} %reshape.499, f32[256]{0:T(256)S(1)} %add_rsqrt_fusion.1, ...), kind=kOutput, calls=%fused_computation.33 | convolution fusion | flops 2155085824 | bytes 15755264 | tf_op jit(solution)/shard_map/dot_general | solution.py:593
  292.9 6.6 fusion.125
  300.9 1.9 fusion.77
  304.1 2.6 convert_reduce_fusion.3
  306.7 7.1 %convert_reduce_fusion.1 = (f32[4096]{0:T(1024)S(1)}, bf16[256,4096]{1,0:T(8,128)(2,1)S(1)}) fusion(f32[256,4096]{1,0:T(8,128)} %get-tuple-element.102, bf16[4096,1024]{1,0:T(8,128)(2,1)} %bitcast.245, f32[256,1024]{1,0:T(8,128)S(1)} %get-tuple-element.66), kind=kOutput, calls=%fused_computation.30 | convolution fusion | flops 2160324608 | bytes 15745024 | tf_op jit(solution)/shard_map/dot_general | solution.py:412
  313.9 6.9 multiply_reduce_fusion.2
  323.7 2.5 reshape.509
  326.2 2.8 copy.73
  328.9 13.4 %multiply_reduce_fusion = (f32[2,16,128]{2,1,0:T(8,128)S(1)}, f32[2,16,128,1024]{3,2,1,0:T(8,128)}) fusion(f32[2,16,128,1024]{3,2,1,0:T(8,128)} %copy-done, f32[2,16,128]{2,1,0:T(8,128)S(1)} %log_add_fusion.1, pred[2,1024]{1,0:T(4,128)(4,1)S(1)} %iota_compare_fusion.1, bf16[2,128,16,64]{1,3,2,0:T(8,128)(2,1)} %copy.73, bf16[2,1024,16,64]{1,0,3,2:T(2,128)(2,1)} %reshape.463), kind=kOutput, calls=%fused_computation.1 | convolution fusion | flops 553644032 | bytes 38307840 | tf_op jit(solution)/shard_map/sqhe,skhe->shqk/dot_general | solution.py:467
  342.3 12.0 %multiply_convert_fusion = bf16[2,16,128,1024]{3,2,1,0:T(8,128)(2,1)S(1)} fusion(f32[2,16,128,1024]{3,2,1,0:T(8,128)} %get-tuple-element.107, f32[2,16,128,1024]{3,2,1,0:T(8,128)} %copy-done, f32[2,16,128]{2,1,0:T(8,128)S(1)} %get-tuple-element.106, f32[2,16,128]{2,1,0:T(8,128)S(1)} %log_add_fusion.1, pred[2,1024]{1,0:T(4,128)(4,1)S(1)} %iota_compare_fusion.1), kind=kLoop, calls=%fused_computation | loop fusion | flops 20971520 | bytes 41977856 | tf_op jit(solution)/shard_map/convert_element_type | solution.py:469
  354.4 8.4 %convert_reduce_fusion.5 = (f32[16,64]{1,0:T(8,128)S(1)}, bf16[2,128,16,64]{1,3,2,0:T(8,128)(2,1)S(1)}) fusion(bf16[2,16,128,1024]{3,2,1,0:T(8,128)(2,1)S(1)} %multiply_convert_fusion, bf16[2,1024,16,64]{1,0,3,2:T(2,128)(2,1)} %reshape.465), kind=kOutput, calls=%fused_computation.111 | convolution fusion | flops 537918464 | bytes 13111296 | tf_op jit(solution)/shard_map/shqk,skhe->sqhe/dot_general | solution.py:470
  363.3 2.6 fusion.36
  371.0 2.0 copy.78
  378.6 3.1 fusion.53
  383.0 6.3 copy.90
  389.3 3.6 copy.113
  393.0 2.2 constant_dynamic-update-slice_fusion.1
  395.2 9.1 %convert_bitcast_fusion = bf16[2,1024,16,64]{1,3,2,0:T(8,128)(2,1)} fusion(bf16[2,128,16,64]{1,3,2,0:T(8,128)(2,1)S(1)} %copy-done.19, f32[2,16,128,1024]{3,2,1,0:T(8,128)} %copy-done, f32[2,16,128]{2,1,0:T(8,128)S(1)} %log_add_fusion.1, pred[2,1024]{1,0:T(4,128)(4,1)S(1)} %iota_compare_fusion.1), kind=kOutput, calls=%fused_computation.31 | convolution fusion | flops 551550976 | bytes 21514240 | tf_op jit(solution)/shard_map/shqk,sqhe->skhe/dot_general | solution.py:476
  404.3 6.5 copy.92
  412.3 2.1 copy-done.1
  414.5 2.3 constant_dynamic-update-slice_fusion
  416.8 12.9 %convolution_convert_fusion.4 = bf16[2048,1024]{1,0:T(8,128)(2,1)} fusion(bf16[2048,2048]{0,1:T(8,128)(2,1)} %constant_dynamic-update-slice_fusion, bf16[1024,3072]{1,0:T(8,128)(2,1)S(1)} %bitcast.230), kind=kOutput, calls=%fused_computation.37 | convolution fusion | flops 8592031744 | bytes 16777216 | tf_op jit(solution)/shard_map/dot_general | solution.py:412
  429.8 5.0 convolution_convert_fusion.2
  434.8 2.1 convolution_convert_fusion.7
  437.3 11.1 %convolution_convert_fusion.3 = bf16[2048,1024]{0,1:T(8,128)(2,1)} fusion(bf16[2048,2048]{0,1:T(8,128)(2,1)S(1)} %copy-done.46, bf16[2048,1024]{1,0:T(8,128)(2,1)S(1)} %bitcast.251), kind=kOutput, calls=%fused_computation.36 | convolution fusion | flops 8592031744 | bytes 16777216 | tf_op jit(solution)/shard_map/dot_general | solution.py:406
  449.3 5.6 pad_maximum_fusion.refs_2_
  455.0 2.1 convolution_convert_fusion.5
  457.4 5.7 convolution_convert_fusion.1
  463.2 5.6 convolution_convert_fusion
  469.9 2.8 convert_reduce_fusion
  474.2 201.3 %scatter_grads.1 = (f32[32,3072]{1,0:T(8,128)}, f32[32,1024]{1,0:T(8,128)}, f32[32,3072]{1,0:T(8,128)}, f32[32,1024]{1,0:T(8,128)}, f32[32,4096]{1,0:T(8,128)}, /*index=5*/f32[128,1024]{1,0:T(8,128)}, f32[8,128]{1,0:T(8,128)}) custom-call(bf16[4,2,2,2,32,3072]{5,4,3,2,1,0:T(8,128)(2,1)} %bitcast.195, bf16[4,2,2,2,32,1024]{5,4,3,2,1,0:T(8,128)(2,1)} %bitcast.203, ...), custom_call_target="tpu_custom_call" | custom-call | tf_op jit(solution)/shard_map/scatter_grads/pallas_call | solution.py:348
  688.1 1.9 copy.213
  (223 shorter events, 52.4 us)
Async XLA Ops:
  209.9 5.7 copy-start.12
  218.3 8.2 %copy-start.50 = (s32[2]{0:T(128)S(1)}, s32[2]{0:T(128)}, u32[]{:S(2)}) copy-start(s32[2]{0:T(128)} %param.25) | copy-start | bytes 28
  218.3 8.4 %copy-start.42 = (bf16[2,128,1024]{2,1,0:T(8,128)(2,1)S(1)}, bf16[2,128,1024]{2,1,0:T(8,128)(2,1)}, u32[]{:S(2)}) copy-start(bf16[2,128,1024]{2,1,0:T(8,128)(2,1)} %param.21) | copy-start | bytes 1572868
  233.3 4.0 copy-start.23
  236.3 2.8 copy-start.25
  238.5 1.9 copy-start.43
  252.4 5.7 copy-start
  271.8 10.6 %copy-start.15 = (bf16[4,2,2,2,32,1024]{5,4,3,2,1,0:T(8,128)(2,1)S(1)}, bf16[4,2,2,2,32,1024]{5,4,3,2,1,0:T(8,128)(2,1)}, u32[]{:S(2)}) copy-start(bf16[4,2,2,2,32,1024]{5,4,3,2,1,0:T(8,128)(2,1)} %get-tuple-element.37) | copy-start | bytes 6291460
  282.4 1.8 copy-start.33
  285.8 7.1 %copy-start.3 = (f32[256,1024]{1,0:T(8,128)S(1)}, f32[256,1024]{1,0:T(8,128)}, u32[]{:S(2)}) copy-start(f32[256,1024]{1,0:T(8,128)} %get-tuple-element.100) | copy-start | bytes 3145732
  292.9 6.6 copy-start.37
  306.7 7.2 %copy-start.35 = (f32[256,1024]{1,0:T(8,128)}, f32[256,1024]{1,0:T(8,128)S(1)}, u32[]{:S(2)}) copy-start(f32[256,1024]{1,0:T(8,128)S(1)} %get-tuple-element.66) | copy-start | bytes 3145732
  306.7 7.2 %copy-start.4 = (f32[256,1024]{1,0:T(8,128)S(1)}, f32[256,1024]{1,0:T(8,128)}, u32[]{:S(2)}) copy-start(f32[256,1024]{1,0:T(8,128)} %get-tuple-element.100) | copy-start | bytes 3145732
  313.9 6.9 %copy-start.40 = (bf16[256,4096]{1,0:T(8,128)(2,1)}, bf16[256,4096]{1,0:T(8,128)(2,1)S(1)}, u32[]{:S(2)}) copy-start(bf16[256,4096]{1,0:T(8,128)(2,1)S(1)} %get-tuple-element.113) | copy-start | bytes 6291460
  313.9 8.3 %copy-start.16 = (bf16[4,2,2,2,32,1024]{5,4,3,2,1,0:T(8,128)(2,1)S(1)}, bf16[4,2,2,2,32,1024]{5,4,3,2,1,0:T(8,128)(2,1)}, u32[]{:S(2)}) copy-start(bf16[4,2,2,2,32,1024]{5,4,3,2,1,0:T(8,128)(2,1)} %get-tuple-element.37) | copy-start | bytes 6291460
  354.4 8.4 %copy-start.2 = (bf16[2,16,128,1024]{3,2,1,0:T(8,128)(2,1)}, bf16[2,16,128,1024]{3,2,1,0:T(8,128)(2,1)S(1)}, u32[]{:S(2)}) copy-start(bf16[2,16,128,1024]{3,2,1,0:T(8,128)(2,1)S(1)} %multiply_convert_fusion) | copy-start | bytes 25165828
  354.4 8.9 %copy-start.7 = (f32[256,1024]{1,0:T(8,128)S(1)}, f32[256,1024]{1,0:T(8,128)}, u32[]{:S(2)}) copy-start(f32[256,1024]{1,0:T(8,128)} %copy-done.6) | copy-start | bytes 3145732
  363.3 3.9 copy-start.27
  363.3 5.2 copy-start.14
  367.6 5.4 copy-start.48
  373.8 1.8 copy-start.26
  373.8 4.8 slice-start.4
  374.9 2.1 copy-start.32
  375.5 2.4 copy-start.29
  375.5 3.1 slice-start.5
  376.4 2.2 copy-start.10
  377.0 4.7 slice-start
  378.6 3.1 copy-start.17
  378.6 3.1 slice-start.1
  378.6 3.1 copy-start.22
  393.0 2.2 copy-start.19
  410.8 5.9 slice-start.2
  412.3 2.1 copy-start.1
  412.3 4.4 slice-start.3
  416.7 13.0 %copy-start.18 = (bf16[256,3072]{0,1:T(8,128)(2,1)S(1)}, bf16[256,3072]{0,1:T(8,128)(2,1)}, u32[]{:S(2)}) copy-start(bf16[256,3072]{0,1:T(8,128)(2,1)} %copy-done.17) | copy-start | bytes 4718596
  416.7 13.0 %copy-start.44 = (bf16[2,128,1024]{2,1,0:T(8,128)(2,1)S(1)}, bf16[2,128,1024]{2,1,0:T(8,128)(2,1)}, u32[]{:S(2)}) copy-start(bf16[2,128,1024]{2,1,0:T(8,128)(2,1)} %param.21) | copy-start | bytes 1572868
  429.7 5.1 copy-start.21
  429.7 7.1 %copy-start.46 = (bf16[2048,2048]{0,1:T(8,128)(2,1)S(1)}, bf16[2048,2048]{0,1:T(8,128)(2,1)}, u32[]{:S(2)}) copy-start(bf16[2048,2048]{0,1:T(8,128)(2,1)} %constant_dynamic-update-slice_fusion) | copy-start | bytes 25165828
  429.7 7.5 %copy-start.49 = (bf16[2,1024,1024]{2,1,0:T(8,128)(2,1)S(1)}, bf16[2,1024,1024]{2,1,0:T(8,128)(2,1)}, u32[]{:S(2)}) copy-start(bf16[2,1024,1024]{2,1,0:T(8,128)(2,1)} %param.22) | copy-start | bytes 12582916
  437.3 11.1 %copy-start.45 = (bf16[1024,256]{0,1:T(8,128)(2,1)S(1)}, bf16[1024,256]{0,1:T(8,128)(2,1)}, u32[]{:S(2)}) copy-start(bf16[1024,256]{0,1:T(8,128)(2,1)} %get-tuple-element.73) | copy-start | bytes 1572868
  437.3 11.3 %copy-start.28 = (bf16[2,128,16,64]{1,0,3,2:T(2,128)(2,1)S(1)}, bf16[2,128,16,64]{1,0,3,2:T(2,128)(2,1)}, u32[]{:S(2)}) copy-start(bf16[2,128,16,64]{1,0,3,2:T(2,128)(2,1)} %copy-done.27) | copy-start | bytes 1572868
  449.3 5.7 copy-start.8
  449.3 5.6 copy-start.34
  455.0 2.1 copy-start.5
  455.0 2.4 copy-start.41
  457.4 5.7 copy-start.36
  457.4 5.7 copy-start.38
  463.2 6.0 copy-start.30
  (9 other events, 11.5 us)
